TPU v7x, 128 devices: a whole 4x4x4 slice. The times are simulated.
128 devices in a mesh: wide: 32 (over z, y, core), narrow: 4 (over x).
Axes of the slice: x: 4, y: 4, z: 4, core: 2. Of those that a mesh axis runs over, the one named last changes fastest.
Arguments:
- face_blocks: float32 [5120, 320, 320], P(('wide', 'narrow')), may hold values from -0.3125 to 0.3125
- face_elems: int32 [5120, 2], P(('wide', 'narrow')), may hold values from 0 to 1023, as said below
- coarse_slot: int32 [1024], replicated, may hold values from 0 to 1023, as said below
- prolong: float32 [320, 135], replicated, may hold values from -0.3125 to 0.3125
- fine_residual: float32 [1024, 320], P(('wide', 'narrow')), may hold values from -6 to 6
- block_inverse: float32 [1024, 135, 135], P(('wide', 'narrow'))
Outputs:
- fine_correction: float32 [1024, 320], P(('wide', 'narrow'))
- owned_blocks: float32 [12288, 135, 135], P(('wide', 'narrow'))
Inputs may be any that keep to these rules, and one draw needn't show every extreme that they name: `coarse_slot`: A permutation: every element has its own coarse row. `face_elems`: the row and column elements of a face differ. With the owner of an element being coarse_slot // 32, among the 40 faces of each device (aligned blocks of 40 rows, devices in the order wide then narrow) at most 3 have row elements of any one owner, and for each narrow index one owner takes exactly 3 faces from every device with that narrow index.
All inputs are finite; a program needn't handle non-finite values.
Results may differ from a plain program's by a relative error of at most 0.000075.
Values sent between devices are 32-bit elements; how exact they have to be, the bound alone decides.
A program may use at most 192 MiB of HBM per device.

v0:
```python
import jax
import jax.numpy as jnp
from jax import lax
from jax.sharding import PartitionSpec as P

DAMPING = 0.7
PRECISE = lax.Precision.HIGHEST


def galerkin(blocks, prolong):
    applied = jnp.einsum("fij,jc->fic", blocks, prolong, precision=PRECISE)
    return jnp.einsum("ia,fic->fac", prolong, applied, precision=PRECISE)


def sum_into_rows(values, targets, rows_total):
    selector = (
        lax.broadcasted_iota(jnp.int32, (rows_total, targets.shape[0]), 0) == targets[None, :]
    ).astype(jnp.float32)
    return jnp.dot(selector, values, precision=PRECISE)


def local(face_blocks, face_elems, coarse_slot, prolong, fine_residual, block_inverse):
    wide_size = lax.axis_size("wide")
    narrow_size = lax.axis_size("narrow")
    dev_rows = fine_residual.shape[0]
    owner_total = dev_rows * narrow_size
    face_total = face_blocks.shape[0]
    coarse_width = prolong.shape[1]
    capacity = max(2, (2 * face_total + wide_size - 1) // wide_size)
    buffer_rows = wide_size * capacity
    coarse_rhs = jnp.dot(fine_residual, prolong, precision=PRECISE)
    sweep_one = DAMPING * jnp.einsum("snm,sm->sn", block_inverse, coarse_rhs, precision=PRECISE)
    iterate_all = lax.all_gather(sweep_one, ("wide", "narrow"), axis=0, tiled=True)
    slot_pairs = jnp.take(coarse_slot, face_elems, axis=0)
    row_slot = slot_pairs[:, 0]
    col_slot = slot_pairs[:, 1]
    target = row_slot // owner_total
    local_row = row_slot % owner_total
    selector = (target[:, None] == jnp.arange(wide_size, dtype=jnp.int32)[None, :]).astype(
        jnp.int32
    )
    ranking = jnp.sum(selector * (jnp.cumsum(selector, axis=0) - 1), axis=1)
    position = target * capacity + ranking
    coarse_blocks = galerkin(face_blocks, prolong)
    send_blocks = (
        jnp.zeros((buffer_rows, coarse_width, coarse_width), jnp.float32)
        .at[position]
        .set(coarse_blocks)
    )
    send_blocks = send_blocks.reshape(wide_size, capacity, coarse_width, coarse_width)
    labels = (
        jnp.zeros((buffer_rows, 2), jnp.int32)
        .at[position]
        .set(jnp.stack([local_row, col_slot], axis=1))
    )
    labels = labels.reshape(wide_size, capacity, 2)
    blocks = lax.all_to_all(send_blocks, "wide", split_axis=0, concat_axis=0, tiled=True)
    labels_in = lax.all_to_all(labels, "wide", split_axis=0, concat_axis=0, tiled=True)
    vectors = jnp.take(iterate_all, labels_in[..., 1], axis=0)
    results = jnp.einsum("wkac,wkc->wka", blocks, vectors, precision=PRECISE)
    targets_in = labels_in[..., 0]
    partial_sums = sum_into_rows(
        results.reshape(-1, coarse_width), targets_in.reshape(-1), owner_total
    )
    coupling = lax.psum_scatter(partial_sums, "narrow", scatter_dimension=0, tiled=True)
    update = (1.0 - DAMPING) * coarse_rhs - coupling
    sweep_two = sweep_one + DAMPING * jnp.einsum(
        "snm,sm->sn", block_inverse, update, precision=PRECISE
    )
    correction = jnp.dot(sweep_two, prolong.T, precision=PRECISE)
    return (correction, blocks.reshape(buffer_rows, coarse_width, coarse_width))


def solution(mesh):
    placed = (
        P(("wide", "narrow"), None, None),
        P(("wide", "narrow"), None),
        P(),
        P(),
        P(("wide", "narrow"), None),
        P(("wide", "narrow"), None, None),
    )
    return jax.shard_map(
        local,
        mesh=mesh,
        in_specs=placed,
        out_specs=(P(("wide", "narrow"), None), P(("wide", "narrow"), None, None)),
        check_vma=False,
    )
```

profile of v0, /device:TPU:0, one launch (start us, length us, event | category | flops | bytes accessed | tf_op | source)
XLA Modules:
  0.0 351.9 jit_solution(5267671407106277412)
XLA Ops:
  7.2 0.7 compare_select_fusion.1
  8.0 0.1 reshape.33
  8.2 1.0 gather_fusion
  9.1 0.1 reshape.32
  9.5 0.2 select_reduce_fusion
  9.8 0.7 scatter_custom_fusion
  10.6 0.1 reshape.27
  10.7 0.6 copy.60
  11.3 8.4 %all-to-all-start = ((s32[32,3,2]{1,2,0:T(2,128)}), s32[32,3,2]{1,2,0:T(2,128)S(1)}, u32[]{:S(2)}, u32[]{:S(2)}) async-start(s32[32,3,2]{1,2,0:T(2,128)} %copy.60), calls=%async_computation | async-start | bytes 65536 | tf_op jit(solution)/shard_map/all_to_all | solution.py:58
  19.8 25.5 %fusion.1 = f32[40,320,135]{1,2,0:T(8,128)S(1)} fusion(f32[40,320,320]{2,1,0:T(8,128)} %param.6, f32[320,135]{0,1:T(8,128)S(1)} %copy-done), kind=kOutput, calls=%fused_computation.6 | convolution fusion | flops 6635520000 | bytes 23468800 | tf_op jit(solution)/shard_map/fij,jc->fic/dot_general | solution.py:11
  45.3 10.7 %convolution_bitcast_fusion = f32[40,135,135]{1,2,0:T(8,128)} fusion(f32[40,320,135]{1,2,0:T(8,128)S(1)} %fusion.1, f32[320,135]{0,1:T(8,128)S(1)} %copy-done), kind=kOutput, calls=%fused_computation.4 | convolution fusion | flops 2799360000 | bytes 10000800 | tf_op jit(solution)/shard_map/ia,fic->fac/dot_general | solution.py:12
  55.9 6.9 %copy.61 = f32[40,135,135]{2,1,0:T(8,128)} copy(f32[40,135,135]{1,2,0:T(8,128)} %convolution_bitcast_fusion) | data formatting | bytes 5832000 | tf_op jit(solution)/shard_map/ia,fic->fac/transpose | solution.py:12
  62.9 5.7 %broadcast_in_dim.31 = f32[96,135,135]{2,1,0:T(8,128)} broadcast(f32[]{:T(128)} %constant.73.clone.1), dimensions={} | broadcast | bytes 6998404 | tf_op jit(solution)/shard_map/broadcast_in_dim | solution.py:46
  68.6 12.1 %scatter_fusion = f32[96,135,135]{2,1,0:T(8,128)} fusion(f32[96,135,135]{2,1,0:T(8,128)} %broadcast_in_dim.31, s32[40]{0:T(128)S(1)} %fusion.19, f32[40,135,135]{2,1,0:T(8,128)} %copy.61), kind=kCustom, calls=%fused_computation.3 | custom fusion | bytes 8748160 | tf_op jit(solution)/shard_map/scatter | solution.py:48
  80.7 7.6 %all-to-all-start.1 = ((f32[32,3,135,135]{3,2,1,0:T(8,128)}), f32[32,3,135,135]{3,2,1,0:T(8,128)}, u32[]{:S(2)}, u32[]{:S(2)}) async-start(f32[32,3,135,135]{3,2,1,0:T(8,128)} %bitcast.46), calls=%async_computation.1 | async-start | bytes 26738688 | tf_op jit(solution)/shard_map/all_to_all | solution.py:57
  88.4 0.7 copy.66
  89.1 0.3 fusion.22
  89.4 0.7 fusion.15
  90.1 217.8 %all_gather.3 = f32[1024,135]{1,0:T(8,128)S(1)} all-gather(f32[8,135]{1,0:T(8,128)S(1)} %bitcast_multiply_fusion.1), channel_id=1, replica_groups=mesh['wide'=32,'narrow'=4] {'wide','narrow'}, dimensions={0}, use_global_device_ids=true | all-gather | bytes 557280 | tf_op jit(solution)/shard_map/all_gather | solution.py:33
  307.9 0.1 slice_reduce_fusion
  308.0 0.1 reshape.41
  308.1 0.7 gather_fusion.1
  309.1 0.1 copy.63
  309.2 0.1 eq.31
  309.3 0.1 select_bitcast_fusion
  309.4 14.0 %fusion.3 = f32[32,3,1,135]{3,2,1,0:T(1,128)S(1)} fusion(f32[32,3,135,135]{3,2,1,0:T(8,128)} %all-to-all-done.1, f32[32,3,135,1]{2,1,0,3:T(4,128)S(1)} %select_bitcast_fusion), kind=kOutput, calls=%fused_computation.10 | convolution fusion | flops 20995200 | bytes 7102080 | tf_op jit(solution)/shard_map/wkac,wkc->wka/dot_general | solution.py:60
  323.5 0.8 fusion.8
  324.3 13.6 %copy.64 = f32[96,135,135]{0,2,1:T(8,128)} copy(f32[96,135,135]{2,1,0:T(8,128)} %bitcast.13) | data formatting | bytes 13996800
  337.9 5.0 %reduce-scatter.2.cloned.1.call-done = f32[8,135]{1,0:T(8,128)} async-done(((f32[32,135]{1,0:T(8,128)}), f32[8,135]{1,0:T(8,128)}) %reduce-scatter.2.cloned.1.call-update) | async-done | bytes 4336 | tf_op jit(solution)/shard_map/reduce_scatter | solution.py:65
  342.9 0.7 subtract_bitcast_fusion
  343.6 0.7 fusion.13
  344.2 0.8 fusion.10
  (33 shorter events, 0.9 us)
Async XLA Ops:
  7.2 12.6 %copy-start = (f32[320,135]{0,1:T(8,128)S(1)}, f32[320,135]{0,1:T(8,128)}, u32[]{:S(2)}) copy-start(f32[320,135]{0,1:T(8,128)} %param.9) | copy-start | bytes 518404
  7.2 1.0 copy-start.1
  8.1 1.2 copy-start.4
  11.3 69.3 %all-to-all-start = ((s32[32,3,2]{1,2,0:T(2,128)}), s32[32,3,2]{1,2,0:T(2,128)S(1)}, u32[]{:S(2)}, u32[]{:S(2)}) async-start(s32[32,3,2]{1,2,0:T(2,128)} %copy.60), calls=%async_computation | async-start | bytes 65536 | tf_op jit(solution)/shard_map/all_to_all | solution.py:58
  80.7 7.7 %copy-start.2 = (f32[8,135,135]{2,0,1:T(8,128)S(1)}, f32[8,135,135]{2,0,1:T(8,128)}, u32[]{:S(2)}) copy-start(f32[8,135,135]{2,0,1:T(8,128)} %param.11) | copy-start | bytes 1749604
  80.7 8.4 %copy-start.3 = (f32[8,320]{1,0:T(8,128)S(1)}, f32[8,320]{1,0:T(8,128)}, u32[]{:S(2)}) copy-start(f32[8,320]{1,0:T(8,128)} %param.10) | copy-start | bytes 30724
  80.7 228.7 %all-to-all-start.1 = ((f32[32,3,135,135]{3,2,1,0:T(8,128)}), f32[32,3,135,135]{3,2,1,0:T(8,128)}, u32[]{:S(2)}, u32[]{:S(2)}) async-start(f32[32,3,135,135]{3,2,1,0:T(8,128)} %bitcast.46), calls=%async_computation.1 | async-start | bytes 26738688 | tf_op jit(solution)/shard_map/all_to_all | solution.py:57
  88.3 254.5 %reduce-scatter.2.cloned.1.call-start = ((), (), s32[]{:S(2)}) async-start(), calls=%async_computation.3 | async-start | bytes 40960 | tf_op jit(solution)/shard_map/reduce_scatter | solution.py:65
Sparse Core Ops, SparseCore 0:
  324.4 18.3 reduce-scatter.1
where the time goes:
time: 353 us; the launch traced here: 352 us
  blocking collectives  218 us (62%)
  matrix products  53.4 us (15%)
  local copies, waits for them, and re-layouts  43.2 us (12%)
  starting transfers between devices  16.1 us (5%)
  between operations  14.3 us (4%)
  waiting for transfers between devices  5.01 us (1%)
    all_gather x1, blocking collectives, local(): lax.all_gather(sweep_one, ('wide', 'narrow'), axis=0, tiled=True)  218 us
    dot_general x1, matrix products, galerkin(): applied = jnp.einsum('fij,jc->fic', blocks, prolong, precision=PRECISE)  25.5 us
    unnamed x12, local copies, waits for them, and re-layouts  14.3 us
    dot_general x1, matrix products, local(): results = jnp.einsum('wkac,wkc->wka', blocks, vectors, precision=PRECISE)  14 us
    scatter x1, local copies, waits for them, and re-layouts, local(): send_blocks = jnp.zeros((buffer_rows, coarse_width, coarse_width), jnp.fl...  12.1 us
    dot_general x1, matrix products, galerkin(): return jnp.einsum('ia,fic->fac', prolong, applied, precision=PRECISE)  10.7 us
    all_to_all x1, starting transfers between devices, local(): lax.all_to_all(labels, 'wide', split_axis=0, concat_axis=0, tiled=True)  8.42 us
    all_to_all x1, starting transfers between devices, local(): lax.all_to_all(send_blocks, 'wide', split_axis=0, concat_axis=0, tiled=True)  7.64 us
  transfers between devices with their start and end apart: 3, of which 1 were waited for; matrix products, arithmetic and copies ran while one was open for 22% of the time, Pallas kernels for 0%

commit v1 on v0

--- a/solution.py
+++ b/solution.py
@@ -30,7 +30,12 @@
     buffer_rows = wide_size * capacity
     coarse_rhs = jnp.dot(fine_residual, prolong, precision=PRECISE)
     sweep_one = DAMPING * jnp.einsum("snm,sm->sn", block_inverse, coarse_rhs, precision=PRECISE)
-    iterate_all = lax.all_gather(sweep_one, ("wide", "narrow"), axis=0, tiled=True)
+    iterate_all = jnp.concatenate(
+        lax.all_to_all(
+            jnp.stack([sweep_one] * lax.axis_size(("wide", "narrow"))), ("wide", "narrow"), 0, 0
+        ),
+        axis=0,
+    )
     slot_pairs = jnp.take(coarse_slot, face_elems, axis=0)
     row_slot = slot_pairs[:, 0]
     col_slot = slot_pairs[:, 1]

time: 353 us -> 317 us (0.90)
  blocking collectives: 218 us -> 0 us
  waiting for transfers between devices: 5.01 us -> 172 us
  starting transfers between devices: 16.1 us -> 26 us
  matrix products: 53.4 us -> 58 us
    all_gather x1 -> x0, blocking collectives: 218 us -> none  [local(): lax.all_gather(sweep_one, ('wide', 'narrow'), axis=0, tiled=True)]
    all_to_all x1, waiting for transfers between devices: 0.01 us -> 169 us  [local(): lax.all_to_all(send_blocks, 'wide', split_axis=0, concat_axis=0, tiled=True)]
    all_to_all x0 -> x1, starting transfers between devices: none -> 10.3 us  [local(): lax.all_to_all(jnp.stack([sweep_one] * lax.axis_size(('wide', 'narrow')))...]
  transfers between devices with their start and end apart: 3 -> 4, of which waited for: 1 -> 2; matrix products, arithmetic and copies ran while one was open for 22% -> 26% of each run, Pallas kernels for 0% -> 0%
where the time goes in v1:
time: 317 us; the launch traced here: 316 us
  waiting for transfers between devices  172 us (54%)
  matrix products  58 us (18%)
  local copies, waits for them, and re-layouts  44.3 us (14%)
  starting transfers between devices  26 us (8%)
  between operations  14.3 us (5%)
    all_to_all x1, waiting for transfers between devices, local(): lax.all_to_all(send_blocks, 'wide', split_axis=0, concat_axis=0, tiled=True)  169 us
    dot_general x1, matrix products, galerkin(): applied = jnp.einsum('fij,jc->fic', blocks, prolong, precision=PRECISE)  27.9 us
    unnamed x12, local copies, waits for them, and re-layouts  14.3 us
    dot_general x1, matrix products, local(): results = jnp.einsum('wkac,wkc->wka', blocks, vectors, precision=PRECISE)  14 us
    dot_general x1, matrix products, galerkin(): return jnp.einsum('ia,fic->fac', prolong, applied, precision=PRECISE)  12.9 us
    scatter x1, local copies, waits for them, and re-layouts, local(): send_blocks = jnp.zeros((buffer_rows, coarse_width, coarse_width), jnp.fl...  12.1 us
    all_to_all x1, starting transfers between devices, local(): lax.all_to_all(jnp.stack([sweep_one] * lax.axis_size(('wide', 'narrow')))...  10.3 us
    all_to_all x1, starting transfers between devices, local(): lax.all_to_all(labels, 'wide', split_axis=0, concat_axis=0, tiled=True)  8.42 us
  transfers between devices with their start and end apart: 4, of which 2 were waited for; matrix products, arithmetic and copies ran while one was open for 26% of the time, Pallas kernels for 0%

profile of v1, /device:TPU:0, one launch (start us, length us, event | category | flops | bytes accessed | tf_op | source)
XLA Modules:
  0.0 316.5 jit_solution(422872557407488975)
XLA Ops:
  7.2 0.7 compare_select_fusion.1
  8.0 0.1 reshape.39
  8.2 1.0 gather_fusion
  9.2 0.1 reshape.38
  9.5 0.2 select_reduce_fusion
  9.8 0.7 scatter_custom_fusion
  10.6 0.1 reshape.32
  10.7 0.6 copy.60
  11.3 8.4 %all-to-all-start = ((s32[32,3,2]{1,2,0:T(2,128)}), s32[32,3,2]{1,2,0:T(2,128)S(1)}, u32[]{:S(2)}, u32[]{:S(2)}) async-start(s32[32,3,2]{1,2,0:T(2,128)} %copy.60), calls=%async_computation | async-start | bytes 65536 | tf_op jit(solution)/shard_map/all_to_all | solution.py:63
  19.8 0.7 copy.66
  20.5 27.9 %fusion.1 = f32[40,320,135]{1,2,0:T(8,128)} fusion(f32[40,320,320]{2,1,0:T(8,128)} %param.6, f32[320,135]{0,1:T(8,128)S(1)} %copy-done), kind=kOutput, calls=%fused_computation.6 | convolution fusion | flops 6635520000 | bytes 23468800 | tf_op jit(solution)/shard_map/fij,jc->fic/dot_general | solution.py:11
  48.4 0.3 fusion.22
  48.6 0.7 fusion.15
  49.4 1.1 stack.5
  50.4 10.3 %all-to-all-start.2 = ((f32[128,8,135]{2,1,0:T(8,128)}), f32[128,8,135]{2,1,0:T(8,128)S(1)}, u32[]{:S(2)}, u32[]{:S(2)}) async-start(f32[128,8,135]{2,1,0:T(8,128)} %stack.5), calls=%async_computation.2 | async-start | bytes 2097152 | tf_op jit(solution)/shard_map/all_to_all | solution.py:34
  60.7 12.9 %convolution_bitcast_fusion = f32[40,135,135]{1,2,0:T(8,128)} fusion(f32[40,320,135]{1,2,0:T(8,128)} %fusion.1, f32[320,135]{0,1:T(8,128)S(1)} %copy-done), kind=kOutput, calls=%fused_computation.4 | convolution fusion | flops 2799360000 | bytes 10000800 | tf_op jit(solution)/shard_map/ia,fic->fac/dot_general | solution.py:12
  73.6 6.9 %copy.61 = f32[40,135,135]{2,1,0:T(8,128)} copy(f32[40,135,135]{1,2,0:T(8,128)} %convolution_bitcast_fusion) | data formatting | bytes 5832000 | tf_op jit(solution)/shard_map/ia,fic->fac/transpose | solution.py:12
  80.5 5.7 %broadcast_in_dim.31 = f32[96,135,135]{2,1,0:T(8,128)} broadcast(f32[]{:T(128)} %constant.73.clone.1), dimensions={} | broadcast | bytes 6998404 | tf_op jit(solution)/shard_map/broadcast_in_dim | solution.py:51
  86.2 12.1 %scatter_fusion = f32[96,135,135]{2,1,0:T(8,128)} fusion(f32[96,135,135]{2,1,0:T(8,128)} %broadcast_in_dim.31, s32[40]{0:T(128)S(1)} %fusion.19, f32[40,135,135]{2,1,0:T(8,128)} %copy.61), kind=kCustom, calls=%fused_computation.3 | custom fusion | bytes 8748160 | tf_op jit(solution)/shard_map/scatter | solution.py:53
  98.3 7.0 %all-to-all-start.1 = ((f32[32,3,135,135]{3,2,1,0:T(8,128)}), f32[32,3,135,135]{3,2,1,0:T(8,128)}, u32[]{:S(2)}, u32[]{:S(2)}) async-start(f32[32,3,135,135]{3,2,1,0:T(8,128)} %bitcast.47), calls=%async_computation.1 | async-start | bytes 26738688 | tf_op jit(solution)/shard_map/all_to_all | solution.py:62
  105.4 0.3 reduce-scatter.2.cloned.1.call-start
  106.0 0.1 copy.63
  106.1 0.1 eq.31
  106.2 0.7 gather_fusion.1
  107.1 168.8 %all-to-all-done.1 = f32[32,3,135,135]{3,2,1,0:T(8,128)} async-done(((f32[32,3,135,135]{3,2,1,0:T(8,128)}), f32[32,3,135,135]{3,2,1,0:T(8,128)}, u32[]{:S(2)}, u32[]{:S(2)}) %all-to-all-start.1) | async-done | bytes 6998432 | tf_op jit(solution)/shard_map/all_to_all | solution.py:62
  275.9 14.0 %fusion.3 = f32[32,3,1,135]{3,2,1,0:T(1,128)S(1)} fusion(f32[32,3,135,135]{3,2,1,0:T(8,128)} %all-to-all-done.1, f32[32,3,135,1]{2,1,0,3:T(4,128)S(1)} %select_bitcast_fusion), kind=kOutput, calls=%fused_computation.10 | convolution fusion | flops 20995200 | bytes 7102080 | tf_op jit(solution)/shard_map/wkac,wkc->wka/dot_general | solution.py:65
  289.9 0.8 fusion.8
  290.7 13.6 %copy.64 = f32[96,135,135]{0,2,1:T(8,128)} copy(f32[96,135,135]{2,1,0:T(8,128)} %bitcast.14) | data formatting | bytes 13996800
  304.3 3.1 reduce-scatter.2.cloned.1.call-done
  307.5 0.7 subtract_bitcast_fusion
  308.2 0.7 fusion.13
  308.8 0.8 fusion.10
  (35 shorter events, 1.2 us)
Async XLA Ops:
  7.2 13.3 %copy-start = (f32[320,135]{0,1:T(8,128)S(1)}, f32[320,135]{0,1:T(8,128)}, u32[]{:S(2)}) copy-start(f32[320,135]{0,1:T(8,128)} %param.9) | copy-start | bytes 518404
  7.2 1.0 copy-start.1
  8.1 1.2 copy-start.4
  8.2 11.6 %copy-start.2 = (f32[8,135,135]{2,0,1:T(8,128)S(1)}, f32[8,135,135]{2,0,1:T(8,128)}, u32[]{:S(2)}) copy-start(f32[8,135,135]{2,0,1:T(8,128)} %param.11) | copy-start | bytes 1749604
  11.3 38.0 %all-to-all-start = ((s32[32,3,2]{1,2,0:T(2,128)}), s32[32,3,2]{1,2,0:T(2,128)S(1)}, u32[]{:S(2)}, u32[]{:S(2)}) async-start(s32[32,3,2]{1,2,0:T(2,128)} %copy.60), calls=%async_computation | async-start | bytes 65536 | tf_op jit(solution)/shard_map/all_to_all | solution.py:63
  20.5 27.9 %copy-start.3 = (f32[8,320]{1,0:T(8,128)S(1)}, f32[8,320]{1,0:T(8,128)}, u32[]{:S(2)}) copy-start(f32[8,320]{1,0:T(8,128)} %param.10) | copy-start | bytes 30724
  50.4 47.9 %all-to-all-start.2 = ((f32[128,8,135]{2,1,0:T(8,128)}), f32[128,8,135]{2,1,0:T(8,128)S(1)}, u32[]{:S(2)}, u32[]{:S(2)}) async-start(f32[128,8,135]{2,1,0:T(8,128)} %stack.5), calls=%async_computation.2 | async-start | bytes 2097152 | tf_op jit(solution)/shard_map/all_to_all | solution.py:34
  98.3 177.5 %all-to-all-start.1 = ((f32[32,3,135,135]{3,2,1,0:T(8,128)}), f32[32,3,135,135]{3,2,1,0:T(8,128)}, u32[]{:S(2)}, u32[]{:S(2)}) async-start(f32[32,3,135,135]{3,2,1,0:T(8,128)} %bitcast.47), calls=%async_computation.1 | async-start | bytes 26738688 | tf_op jit(solution)/shard_map/all_to_all | solution.py:62
  105.4 202.1 %reduce-scatter.2.cloned.1.call-start = ((), (), s32[]{:S(2)}) async-start(), calls=%async_computation.4 | async-start | bytes 40960 | tf_op jit(solution)/shard_map/reduce_scatter | solution.py:70
Sparse Core Ops, SparseCore 0:
  290.9 16.5 reduce-scatter.1
